TPU v7x, 32 devices: a whole 2x2x4 slice. The times are simulated.
32 devices in a mesh: row: 4 (over y, x), col: 8 (over z, core).
Axes of the slice: x: 2, y: 2, z: 4, core: 2. Of those that a mesh axis runs over, the one named last changes fastest.
Arguments:
- front: float32 [16, 1024, 8, 2048], P(None, 'row', None, 'col'), may hold values from -6 to 6
- children: float32 [8, 4096, 4096], P('row', None, 'col'), may hold values from -6 to 6
- child_rows: int32 [8, 16], replicated, may hold values from 0 to 63, as said below
- owner_slots: int32 [8], replicated, may hold values from 0 to 1, as said below
- inverses: float32 [3, 256, 256], replicated, may hold values from -0.0390625 to 0.0390625
- pattern: int32 [64, 64], replicated, may hold values 0 or 1
Outputs:
- factored: float32 [16, 1024, 8, 2048], P(None, 'row', None, 'col')
Inputs may be any that keep to these rules, and one draw needn't show every extreme that they name: `child_rows`: the 16 entries of one slot are distinct. For each slot g there is an offset o_g such that entry k taken mod 8 equals (k // (16 / 8) + o_g) mod 8, and every offset 0 to 8 - 1 belongs to exactly 8 / 8 slots. Hence each residue mod 4 appears exactly 16 / 4 times in each slot. `owner_slots`: slots g = o * 2 + s belong to owner o; an owner's live slots come first, slot 0 of every owner is live, at least one owner has all 2 slots live and at least one other owner has fewer.
All inputs are finite; a program needn't handle non-finite values.
Results may differ from a plain program's by a relative error of at most 0.00014.
Values sent between devices are 32-bit elements; how exact they have to be, the bound alone decides.
A program may use at most 320 MiB of HBM per device.

v0:
```python
import jax
import jax.numpy as jnp
from jax import lax
from jax.sharding import PartitionSpec as P

precise = lax.Precision.HIGHEST


def from_root(block, axis, holder):
    block = jnp.where(lax.axis_index(axis) == holder, block, jnp.zeros_like(block))
    return lax.psum(block, axis)


def shards(front, children, child_rows, owner_slots, inverses, pattern):
    rows_n = lax.axis_size("row")
    cols_n = lax.axis_size("col")
    my_row = lax.axis_index("row")
    my_col = lax.axis_index("col")
    local_rows, tile_size, local_cols, _ = front.shape
    slots_here, child_order, child_width = children.shape
    kblocks = child_order // tile_size
    per_row = kblocks // rows_n
    per_col = child_width // tile_size
    slot_total = child_rows.shape[0]
    per_dest = slot_total // cols_n
    panel_count = inverses.shape[0]
    col_ratio = cols_n // rows_n
    position = jnp.arange(kblocks, dtype=jnp.int32)
    row_order = jnp.argsort(child_rows % rows_n * kblocks + position[None, :], axis=1)
    my_order = lax.dynamic_slice_in_dim(row_order, my_row * slots_here, slots_here, 0)
    my_rank = lax.dynamic_slice_in_dim(row_order, my_row * per_row, per_row, 1)
    row_blocks = jnp.take_along_axis(child_rows, my_rank, axis=1)
    col_blocks = child_rows.reshape(slot_total, cols_n, per_col)
    slot_ids = jnp.arange(slot_total, dtype=jnp.int32)
    local_row_ids = jnp.arange(local_rows, dtype=jnp.int32)
    local_col_ids = jnp.arange(local_cols, dtype=jnp.int32)
    blocks_in = children.reshape(slots_here, kblocks, tile_size, child_width)
    sorted_rows = jnp.take_along_axis(blocks_in, my_order[:, :, None, None], axis=1)
    outgoing = sorted_rows.reshape(slots_here, rows_n, per_row, tile_size, child_width)
    arrived = lax.all_to_all(outgoing, "row", split_axis=1, concat_axis=0, tiled=True)
    arrived = arrived.reshape(slot_total, per_row, tile_size, child_width)
    dest_by_src = jnp.transpose(col_blocks[:, :, 0] % cols_n)
    send_order = jnp.argsort(dest_by_src * slot_total + slot_ids[None, :], axis=1)
    my_send = lax.dynamic_index_in_dim(send_order, my_col, 0, keepdims=False)
    outgoing = jnp.take(arrived, my_send, axis=0).reshape(
        cols_n, per_dest, per_row, tile_size, child_width
    )
    landed = lax.all_to_all(outgoing, "col", split_axis=0, concat_axis=0, tiled=True)
    recv_slot = lax.dynamic_slice_in_dim(send_order, my_col * per_dest, per_dest, 1)
    got_rows = row_blocks[recv_slot]
    src_ids = jnp.arange(cols_n, dtype=jnp.int32)
    got_cols = col_blocks[recv_slot, src_ids[:, None]]
    live_flag = owner_slots[recv_slot].astype(jnp.float32)
    row_hits = ((got_rows // rows_n)[..., None] == local_row_ids).astype(jnp.float32)
    row_hits = row_hits * live_flag[:, :, None, None]
    col_hits = ((got_cols // cols_n)[..., None] == local_col_ids).astype(jnp.float32)
    pieces = landed.reshape(cols_n, per_dest, per_row, tile_size, per_col, tile_size)
    extend_sum = jnp.einsum("snpa,sntb,snpxty->axby", row_hits, col_hits, pieces, precision=precise)
    summed_front = front + extend_sum
    block_index = local_row_ids * rows_n + my_row
    col_index = local_col_ids * cols_n + my_col
    top_index = my_col // rows_n
    top_root = my_col % rows_n
    current = summed_front[:, :, 0, :]
    factors = []
    for step_index in range(panel_count):
        column = from_root(current, "col", step_index)
        factor = jnp.einsum("axy,zy->axz", column, inverses[step_index], precision=precise)
        factor = jnp.where(
            (block_index >= step_index)[:, None, None], factor, jnp.zeros_like(factor)
        )
        factors.append(factor)
        if step_index + 1 < panel_count:
            top_block = lax.dynamic_index_in_dim(factor, top_index, 0, keepdims=False)
            top_block = from_root(top_block, "row", top_root)
            reduced = current - jnp.einsum("axy,zy->axz", factor, top_block, precision=precise)
            current = jnp.where(my_col > step_index, reduced, current)
    lower = jnp.concatenate(factors, axis=2)
    lower_split = lower.reshape(local_cols, col_ratio, tile_size, panel_count * tile_size)
    chosen = lax.dynamic_index_in_dim(lower_split, top_index, 1, keepdims=False)
    across = from_root(chosen, "row", top_root)
    trailing_sum = jnp.einsum("axk,byk->axby", lower, across, precision=precise)
    block_mask = pattern.reshape(local_rows, rows_n, local_cols, cols_n)
    block_mask = lax.dynamic_index_in_dim(block_mask, my_row, 1, keepdims=False)
    block_mask = lax.dynamic_index_in_dim(block_mask, my_col, 2, keepdims=False)
    trailing = (
        (block_mask > 0)
        & (block_index >= panel_count)[:, None]
        & (col_index >= panel_count)[None, :]
    )
    result = jnp.where(trailing[:, None, :, None], summed_front - trailing_sum, summed_front)
    stacked = jnp.stack(factors, axis=0)
    mine_factor = lax.dynamic_index_in_dim(
        stacked, jnp.minimum(my_col, panel_count - 1), 0, keepdims=False
    )
    first_col = jnp.where(my_col < panel_count, mine_factor, result[:, :, 0, :])
    result = result.at[:, :, 0, :].set(first_col)
    return result


def solution(mesh):
    return jax.shard_map(
        shards,
        mesh=mesh,
        in_specs=(P(None, "row", None, "col"), P("row", None, "col"), P(), P(), P(), P()),
        out_specs=P(None, "row", None, "col"),
        check_vma=False,
    )
```

profile of v0, /device:TPU:0, one launch (start us, length us, event | category | flops | bytes accessed | tf_op | source)
XLA Modules:
  0.0 1667.9 jit_solution(10317902727512108828)
XLA Ops:
  6.5 0.8 copy.149
  7.3 0.7 sort.35
  8.5 14.7 gather_fusion.4
  23.1 7.7 broadcast_select_fusion
  30.9 7.5 copy.156
  38.4 7.0 all-to-all-start
  45.5 0.6 sort.34
  46.3 182.8 %all-to-all-done = f32[2,4,4,256,512]{4,3,2,0,1:T(8,128)} async-done(((f32[2,4,4,256,512]{4,3,2,0,1:T(8,128)}), f32[2,4,4,256,512]{4,3,2,0,1:T(8,128)}, u32[]{:S(2)}, u32[]{:S(2)}) %all-to-all-start) | async-done | bytes 16777248 | tf_op jit(solution)/shard_map/all_to_all | solution.py:40
  229.1 14.2 gather_fusion
  243.3 12.3 fusion.2
  255.6 5.9 all-to-all-start.1
  262.0 0.6 gather_fusion.2
  263.0 0.7 gather_fusion.5
  265.1 360.1 %all-to-all-done.1 = f32[8,1,4,256,512]{4,3,2,1,0:T(8,128)} async-done(((f32[8,1,4,256,512]{4,3,2,1,0:T(8,128)}), f32[8,1,4,256,512]{4,3,2,1,0:T(8,128)}, u32[]{:S(2)}, u32[]{:S(2)}) %all-to-all-start.1) | async-done | bytes 16777248 | tf_op jit(solution)/shard_map/all_to_all | solution.py:48
  625.2 17.4 %copy.158 = f32[8,1,4,256,512]{3,4,2,0,1:T(8,128)} copy(f32[8,1,4,256,512]{4,3,2,1,0:T(8,128)} %all-to-all-done.1) | data formatting | bytes 33554432 | tf_op jit(solution)/shard_map/all_to_all | solution.py:48
  642.5 19.8 %copy.162 = f32[8,4,256,2,256]{4,1,3,2,0:T(4,128)} copy(f32[8,4,256,2,256]{2,4,3,1,0:T(8,128)} %bitcast.125) | data formatting | bytes 33554432 | tf_op jit(solution)/shard_map/reshape.50
  662.4 59.5 %fusion.20 = f32[8,256,2,256,16]{3,4,2,1,0:T(8,128)} fusion(f32[8,4,256,2,256]{4,1,3,2,0:T(4,128)} %copy.162, f32[8]{0:T(128)S(1)} %convert_element_type.16, s32[8,4]{1,0:T(8,128)S(1)} %add_select_fusion.2), kind=kOutput, calls=%fused_computation.46 | convolution fusion | flops 805307392 | bytes 83886240 | tf_op jit(solution)/shard_map/snpa,sntb,snpxty->axby/dot_general | solution.py:58
  721.9 78.1 %bitcast_add_fusion = f32[16,256,8,256]{3,2,0,1:T(8,128)} fusion(f32[16,256,8,256]{3,2,1,0:T(8,128)} %param.8, f32[8,256,2,256,16]{3,4,2,1,0:T(8,128)} %fusion.20, s32[8,2]{0,1:T(2,128)S(1)} %copy.164), kind=kOutput, calls=%fused_computation.9 | convolution fusion | flops 1619001472 | bytes 134217792 | tf_op jit(solution)/shard_map/snpa,sntb,snpxty->axby/dot_general | solution.py:58
  799.9 12.2 slice.62
  812.2 1.9 copy-done.8
  814.1 2.5 bitcast_select_fusion.1
  816.7 94.5 %all-reduce.7.cloned.1.call-done = f32[16,256,256]{2,0,1:T(8,128)} async-done(((f32[16,256,256]{2,0,1:T(8,128)}), f32[16,256,256]{2,0,1:T(8,128)}) %all-reduce.7.cloned.1.call-update) | async-done | bytes 4194320 | tf_op jit(solution)/shard_map/psum | solution.py:11
  911.2 5.4 convolution_select_fusion.2
  916.7 2.0 copy-done.5
  918.9 0.7 copy.217
  920.1 42.7 %all-reduce.9.cloned.1.call-done = f32[256,256]{1,0:T(8,128)} async-done(((f32[256,256]{1,0:T(8,128)}), f32[256,256]{1,0:T(8,128)}) %all-reduce.9.cloned.1.call-update) | async-done | bytes 262160 | tf_op jit(solution)/shard_map/psum | solution.py:11
  962.8 10.3 broadcast_select_fusion.2
  973.2 96.6 %all-reduce.11.cloned.1.call-done = f32[16,256,256]{2,0,1:T(8,128)} async-done(((f32[16,256,256]{2,0,1:T(8,128)}), f32[16,256,256]{2,0,1:T(8,128)}) %all-reduce.11.cloned.1.call-update) | async-done | bytes 4194320 | tf_op jit(solution)/shard_map/psum | solution.py:11
  1069.8 5.4 convolution_select_fusion.1
  1075.2 2.1 copy-done.3
  1077.5 0.7 copy.216
  1078.3 43.1 %all-reduce.13.cloned.1.call-done = f32[256,256]{1,0:T(8,128)} async-done(((f32[256,256]{1,0:T(8,128)}), f32[256,256]{1,0:T(8,128)}) %all-reduce.13.cloned.1.call-update) | async-done | bytes 262160 | tf_op jit(solution)/shard_map/psum | solution.py:11
  1121.4 8.9 fusion.9
  1130.6 96.4 %all-reduce.15.cloned.1.call-done = f32[16,256,256]{2,0,1:T(8,128)} async-done(((f32[16,256,256]{2,0,1:T(8,128)}), f32[16,256,256]{2,0,1:T(8,128)}) %all-reduce.15.cloned.1.call-update) | async-done | bytes 4194320 | tf_op jit(solution)/shard_map/psum | solution.py:11
  1227.0 5.6 convolution_select_fusion
  1232.6 1.9 copy-done.7
  1234.5 4.9 pad_maximum_fusion
  1239.4 15.1 reshape.317
  1254.5 8.6 constant_dynamic-slice_fusion
  1263.1 5.1 fusion.7
  1268.2 0.7 copy-done.10
  1269.5 5.9 fusion.11
  1275.3 131.5 %all-reduce.17.cloned.1.call-done = f32[8,256,768]{2,1,0:T(8,128)} async-done(((f32[8,256,768]{2,1,0:T(8,128)}), f32[8,256,768]{2,1,0:T(8,128)}) %all-reduce.17.cloned.1.call-update) | async-done | bytes 6291472 | tf_op jit(solution)/shard_map/psum | solution.py:11
  1406.8 86.7 %fusion.5 = f32[16,256,8,256]{3,0,2,1:T(8,128)} fusion(f32[8,256,768]{2,1,0:T(8,128)} %all-reduce.17.cloned.1.call-done, f32[16,256,256]{2,0,1:T(8,128)} %copy-done.7, f32[16,256,256]{2,0,1:T(8,128)} %copy-done.3, f32[16,256,256]{2,0,1:T(8,128)} %copy-done.5), kind=kOutput, calls=%fused_computation.16 | convolution fusion | flops 77315702784 | bytes 52428800 | tf_op jit(solution)/shard_map/axk,byk->axby/dot_general | solution.py:82
  1493.5 38.4 %subtract_select_fusion = f32[16,256,8,256]{3,2,0,1:T(8,128)} fusion(f32[16,256,8,256]{3,2,0,1:T(8,128)} %bitcast_add_fusion, f32[16,256,8,256]{3,0,2,1:T(8,128)} %fusion.5, pred[16,8]{1,0:T(8,128)(4,1)S(1)} %copy.148), kind=kLoop, calls=%fused_computation.8 | loop fusion | flops 16777216 | bytes 100663424 | tf_op jit(solution)/shard_map/jit(_where)/select_n | solution.py:91
  1531.9 15.2 broadcast_select_fusion.1
  1547.1 90.7 %scatter.4 = f32[16,256,8,256]{3,2,0,1:T(8,128)} dynamic-update-slice(f32[16,256,8,256]{3,2,0,1:T(8,128)} %subtract_select_fusion, f32[16,256,1,256]{3,2,0,1:T(1,128)} %broadcast_select_fusion.1, s32[]{:T(128)} %constant.195.clone.1, s32[]{:T(128)} %constant.195.clone.1, s32[]{:T(128)} %constant.195.clone.1, s32[]{:T(128)} %constant.195.clone.1) | dynamic-update-slice | bytes 8388612 | tf_op jit(solution)/shard_map/scatter | solution.py:97
  1637.8 22.9 %copy.178 = f32[16,256,8,256]{3,2,1,0:T(8,128)} copy(f32[16,256,8,256]{3,2,0,1:T(8,128)} %scatter.4) | data formatting | bytes 67108864 | tf_op jit(solution)/shard_map/scatter | solution.py:97
  (78 shorter events, 5.0 us)
Async XLA Ops:
  6.5 255.4 %copy-start = (s32[8]{0:T(128)S(1)}, s32[8]{0:T(128)}, u32[]{:S(2)}) copy-start(s32[8]{0:T(128)} %param.11) | copy-start | bytes 100
  38.4 190.7 %all-to-all-start = ((f32[2,4,4,256,512]{4,3,2,0,1:T(8,128)}), f32[2,4,4,256,512]{4,3,2,0,1:T(8,128)}, u32[]{:S(2)}, u32[]{:S(2)}) async-start(f32[2,4,4,256,512]{4,3,2,0,1:T(8,128)} %copy.156), calls=%async_computation | async-start | bytes 33554432 | tf_op jit(solution)/shard_map/all_to_all | solution.py:40
  255.6 7.4 copy-start.2
  255.6 369.6 %all-to-all-start.1 = ((f32[8,1,4,256,512]{4,3,2,1,0:T(8,128)}), f32[8,1,4,256,512]{4,3,2,1,0:T(8,128)}, u32[]{:S(2)}, u32[]{:S(2)}) async-start(f32[8,1,4,256,512]{4,3,2,1,0:T(8,128)} %fusion.2), calls=%async_computation.1 | async-start | bytes 33554432 | tf_op jit(solution)/shard_map/all_to_all | solution.py:48
  261.5 649.7 %all-reduce.7.cloned.1.call-start = ((), (), s32[]{:S(2)}) async-start(), calls=%async_computation.2 | async-start | bytes 8388608 | tf_op jit(solution)/shard_map/psum | solution.py:11
  812.2 1.9 copy-start.8
  816.6 94.6 %copy-start.9 = (f32[3,256,256]{2,1,0:T(8,128)S(1)}, f32[3,256,256]{2,1,0:T(8,128)}, u32[]{:S(2)}) copy-start(f32[3,256,256]{2,1,0:T(8,128)} %param.12) | copy-start | bytes 2359300
  816.6 146.2 %all-reduce.9.cloned.1.call-start = ((), (), s32[]{:S(2)}) async-start(), calls=%async_computation.3 | async-start | bytes 524288 | tf_op jit(solution)/shard_map/psum | solution.py:11
  916.6 2.0 copy-start.5
  919.6 150.1 %all-reduce.11.cloned.1.call-start = ((), (), s32[]{:S(2)}) async-start(), calls=%async_computation.4 | async-start | bytes 8388608 | tf_op jit(solution)/shard_map/psum | solution.py:11
  973.1 148.3 %all-reduce.13.cloned.1.call-start = ((), (), s32[]{:S(2)}) async-start(), calls=%async_computation.5 | async-start | bytes 524288 | tf_op jit(solution)/shard_map/psum | solution.py:11
  1075.2 2.1 copy-start.3
  1078.3 148.7 %all-reduce.15.cloned.1.call-start = ((), (), s32[]{:S(2)}) async-start(), calls=%async_computation.6 | async-start | bytes 8388608 | tf_op jit(solution)/shard_map/psum | solution.py:11
  1130.4 276.5 %all-reduce.17.cloned.1.call-start = ((), (), s32[]{:S(2)}) async-start(), calls=%async_computation.7 | async-start | bytes 12582912 | tf_op jit(solution)/shard_map/psum | solution.py:11
  1227.0 7.5 copy-start.4
  1227.0 7.5 copy-start.6
  1232.6 1.9 copy-start.7
  1268.2 0.8 copy-start.10
  1637.8 22.9 %copy-start.1 = (s32[8]{0:T(128)S(1)}, s32[8]{0:T(128)}, u32[]{:S(2)}) copy-start(s32[8]{0:T(128)} %param.11) | copy-start | bytes 100
Sparse Core Ops, SparseCore 0:
  816.7 94.4 all-reduce.6
  919.8 42.9 all-reduce.8
  973.2 96.5 all-reduce.10
  1078.4 42.9 all-reduce.12
  1130.5 96.4 all-reduce.14
  1268.3 138.4 all-reduce.16
where the time goes:
time: 1680 us; the launch traced here: 1670 us
  waiting for transfers between devices  1050 us (62%)
  matrix products  260 us (15%)
  local copies, waits for them, and re-layouts  238 us (14%)
  other arithmetic  94.4 us (6%)
    psum x6, waiting for transfers between devices, from_root(): return lax.psum(block, axis)  505 us
    all_to_all x1, waiting for transfers between devices, shards(): lax.all_to_all(outgoing, 'col', split_axis=0, concat_axis=0, tiled=True)  360 us
    all_to_all x1, waiting for transfers between devices, shards(): lax.all_to_all(outgoing, 'row', split_axis=1, concat_axis=0, tiled=True)  183 us
    dot_general x2, matrix products, shards(): jnp.einsum('snpa,sntb,snpxty->axby', row_hits, col_hits, pieces, precisio...  138 us
    scatter x2, local copies, waits for them, and re-layouts, shards(): result = result.at[:, :, 0, :].set(first_col)  114 us
    dot_general x1, matrix products, shards(): trailing_sum = jnp.einsum('axk,byk->axby', lower, across, precision=precise)  86.7 us
    select_n x1, other arithmetic, shards(): jnp.where(trailing[:, None, :, None], summed_front - trailing_sum, summed...  38.4 us
  transfers between devices with their start and end apart: 8, of which 8 were waited for; matrix products, arithmetic and copies ran while one was open for 1% of the time, Pallas kernels for 0%

commit v1 on v0

--- a/solution.py
+++ b/solution.py
@@ -8,7 +8,7 @@
 
 def from_root(block, axis, holder):
     block = jnp.where(lax.axis_index(axis) == holder, block, jnp.zeros_like(block))
-    return lax.psum(block, axis)
+    return jnp.sum(lax.all_gather(block, axis), axis=0)
 
 
 def shards(front, children, child_rows, owner_slots, inverses, pattern):

time: 1680 us -> 2400 us (1.43)
  waiting for transfers between devices: 1050 us -> 1670 us
  other arithmetic: 94.4 us -> 184 us
    all_gather x0 -> x6, waiting for transfers between devices: none -> 1130 us  [from_root(): return jnp.sum(lax.all_gather(block, axis), axis=0)]
    psum x6 -> x0, waiting for transfers between devices: 505 us -> none  [from_root(): return lax.psum(block, axis)]
    reduce_sum x0 -> x6, other arithmetic: none -> 69.3 us  [from_root(): return jnp.sum(lax.all_gather(block, axis), axis=0)]
  transfers between devices with their start and end apart: 8 -> 8, of which waited for: 8 -> 8; matrix products, arithmetic and copies ran while one was open for 1% -> 0% of each run, Pallas kernels for 0% -> 0%
where the time goes in v1:
time: 2400 us; the launch traced here: 2390 us
  waiting for transfers between devices  1670 us (70%)
  matrix products  261 us (11%)
  local copies, waits for them, and re-layouts  240 us (10%)
  other arithmetic  184 us (8%)
    all_gather x6, waiting for transfers between devices, from_root(): return jnp.sum(lax.all_gather(block, axis), axis=0)  1130 us
    all_to_all x1, waiting for transfers between devices, shards(): lax.all_to_all(outgoing, 'col', split_axis=0, concat_axis=0, tiled=True)  360 us
    all_to_all x1, waiting for transfers between devices, shards(): lax.all_to_all(outgoing, 'row', split_axis=1, concat_axis=0, tiled=True)  183 us
    dot_general x2, matrix products, shards(): jnp.einsum('snpa,sntb,snpxty->axby', row_hits, col_hits, pieces, precisio...  138 us
    scatter x2, local copies, waits for them, and re-layouts, shards(): result = result.at[:, :, 0, :].set(first_col)  114 us
    dot_general x1, matrix products, shards(): trailing_sum = jnp.einsum('axk,byk->axby', lower, across, precision=precise)  87.7 us
    reduce_sum x6, other arithmetic, from_root(): return jnp.sum(lax.all_gather(block, axis), axis=0)  69.3 us
  transfers between devices with their start and end apart: 8, of which 8 were waited for; matrix products, arithmetic and copies ran while one was open for 0% of the time, Pallas kernels for 0%

profile of v1, /device:TPU:0, one launch (start us, length us, event | category | flops | bytes accessed | tf_op | source)
XLA Modules:
  0.0 2388.1 jit_solution(16721462905899593699)
XLA Ops:
  6.5 0.8 copy.145
  8.5 14.7 gather_fusion.4
  23.1 7.7 broadcast_select_fusion.1
  30.9 7.5 copy.152
  38.4 7.0 all-to-all-start
  46.3 182.8 %all-to-all-done = f32[2,4,4,256,512]{4,3,2,0,1:T(8,128)} async-done(((f32[2,4,4,256,512]{4,3,2,0,1:T(8,128)}), f32[2,4,4,256,512]{4,3,2,0,1:T(8,128)}, u32[]{:S(2)}, u32[]{:S(2)}) %all-to-all-start) | async-done | bytes 16777248 | tf_op jit(solution)/shard_map/all_to_all | solution.py:40
  229.1 14.2 gather_fusion
  243.3 12.3 fusion.2
  255.6 5.9 all-to-all-start.1
  265.2 359.9 %all-to-all-done.1 = f32[8,1,4,256,512]{4,3,2,1,0:T(8,128)} async-done(((f32[8,1,4,256,512]{4,3,2,1,0:T(8,128)}), f32[8,1,4,256,512]{4,3,2,1,0:T(8,128)}, u32[]{:S(2)}, u32[]{:S(2)}) %all-to-all-start.1) | async-done | bytes 16777248 | tf_op jit(solution)/shard_map/all_to_all | solution.py:48
  625.2 17.4 copy.154
  642.5 19.8 copy.158
  662.4 59.5 %fusion.20 = f32[8,256,2,256,16]{3,4,2,1,0:T(8,128)} fusion(f32[8,4,256,2,256]{4,1,3,2,0:T(4,128)} %copy.158, f32[8]{0:T(128)S(1)} %convert_element_type.16, s32[8,4]{1,0:T(8,128)S(1)} %add_select_fusion.2), kind=kOutput, calls=%fused_computation.45 | convolution fusion | flops 805307392 | bytes 83886240 | tf_op jit(solution)/shard_map/snpa,sntb,snpxty->axby/dot_general | solution.py:58
  721.9 78.4 %bitcast_add_fusion = f32[16,256,8,256]{3,2,0,1:T(8,128)} fusion(f32[16,256,8,256]{3,2,1,0:T(8,128)} %param.8, f32[8,256,2,256,16]{3,4,2,1,0:T(8,128)} %fusion.20, s32[8,2]{0,1:T(2,128)S(1)} %copy.160), kind=kOutput, calls=%fused_computation.9 | convolution fusion | flops 1619001472 | bytes 134217792 | tf_op jit(solution)/shard_map/snpa,sntb,snpxty->axby/dot_general | solution.py:58
  800.2 17.7 broadcast_select_fusion.3
  818.0 286.6 %all-gather.15.cloned.1.call-done = f32[128,256,1,256]{3,2,0,1:T(1,128)} async-done(((f32[16,256,1,256]{3,2,0,1:T(1,128)}), f32[128,256,1,256]{3,2,0,1:T(1,128)}) %all-gather.15.cloned.1.call-update) | async-done | bytes 33554448 | tf_op jit(solution)/shard_map/all_gather | solution.py:11
  1104.6 25.1 %copy.198 = f32[128,256,1,256]{3,0,2,1:T(8,128)} copy(f32[128,256,1,256]{3,2,0,1:T(1,128)} %all-gather.15.cloned.1.call-done) | data formatting | bytes 67108864
  1129.8 15.2 reduce_sum.54
  1145.0 5.4 convolution_select_fusion.2
  1150.4 2.0 copy-done.6
  1152.6 0.7 copy.165
  1153.4 24.9 %all-gather.11.cloned.1.call-done = f32[4,256,256]{2,1,0:T(8,128)} async-done(((f32[1,256,256]{2,1,0:T(8,128)}), f32[4,256,256]{2,1,0:T(8,128)}) %all-gather.11.cloned.1.call-update) | async-done | bytes 1048592 | tf_op jit(solution)/shard_map/all_gather | solution.py:11
  1178.4 1.3 reduce_sum.55
  1179.7 10.3 broadcast_select_fusion.4
  1190.1 288.7 %all-gather.17.cloned.1.call-done = f32[128,256,256]{2,0,1:T(8,128)} async-done(((f32[16,256,256]{2,0,1:T(8,128)}), f32[128,256,256]{2,0,1:T(8,128)}) %all-gather.17.cloned.1.call-update) | async-done | bytes 33554448 | tf_op jit(solution)/shard_map/all_gather | solution.py:11
  1478.8 15.4 reduce_sum.56
  1494.2 5.4 convolution_select_fusion.1
  1499.6 2.1 copy-done.3
  1502.0 0.7 copy.170
  1503.2 24.5 %all-gather.13.cloned.1.call-done = f32[4,256,256]{2,1,0:T(8,128)} async-done(((f32[1,256,256]{2,1,0:T(8,128)}), f32[4,256,256]{2,1,0:T(8,128)}) %all-gather.13.cloned.1.call-update) | async-done | bytes 1048592 | tf_op jit(solution)/shard_map/all_gather | solution.py:11
  1527.7 1.3 reduce_sum.57
  1529.0 8.9 fusion.9
  1538.0 288.7 %all-gather.19.cloned.1.call-done = f32[128,256,256]{2,0,1:T(8,128)} async-done(((f32[16,256,256]{2,0,1:T(8,128)}), f32[128,256,256]{2,0,1:T(8,128)}) %all-gather.19.cloned.1.call-update) | async-done | bytes 33554448 | tf_op jit(solution)/shard_map/all_gather | solution.py:11
  1826.7 15.3 reduce_sum.58
  1842.0 5.6 convolution_select_fusion
  1847.6 1.9 copy-done.9
  1849.5 4.8 pad_maximum_fusion
  1854.3 15.1 reshape.334
  1869.4 10.1 broadcast_select_fusion
  1879.6 0.7 copy-done.11
  1880.8 6.7 fusion.11
  1887.5 218.1 %all-gather.21.cloned.1.call-done = f32[32,1,256,768]{3,1,0,2:T(1,128)} async-done(((f32[8,1,256,768]{3,1,0,2:T(1,128)}), f32[32,1,256,768]{3,1,0,2:T(1,128)}) %all-gather.21.cloned.1.call-update) | async-done | bytes 25165840 | tf_op jit(solution)/shard_map/all_gather | solution.py:11
  2105.6 20.7 bitcast_reduce_fusion
  2126.3 87.7 %fusion.5 = f32[16,256,8,256]{3,0,2,1:T(8,128)} fusion(f32[8,256,768]{2,0,1:T(8,128)} %bitcast_reduce_fusion, f32[16,256,256]{2,0,1:T(8,128)} %copy-done.9, f32[16,256,256]{2,0,1:T(8,128)S(1)} %copy-done.5, f32[16,256,256]{2,0,1:T(8,128)S(1)} %copy-done.8), kind=kOutput, calls=%fused_computation.17 | convolution fusion | flops 77315702784 | bytes 52428800 | tf_op jit(solution)/shard_map/axk,byk->axby/dot_general | solution.py:82
  2214.0 38.1 %subtract_select_fusion = f32[16,256,8,256]{3,2,0,1:T(8,128)} fusion(f32[16,256,8,256]{3,2,0,1:T(8,128)} %bitcast_add_fusion, f32[16,256,8,256]{3,0,2,1:T(8,128)} %fusion.5, pred[16,8]{1,0:T(8,128)(4,1)S(1)} %copy.144), kind=kLoop, calls=%fused_computation.8 | loop fusion | flops 16777216 | bytes 100663424 | tf_op jit(solution)/shard_map/jit(_where)/select_n | solution.py:91
  2252.1 15.2 broadcast_select_fusion.2
  2267.3 90.7 %scatter.4 = f32[16,256,8,256]{3,2,0,1:T(8,128)} dynamic-update-slice(f32[16,256,8,256]{3,2,0,1:T(8,128)} %subtract_select_fusion, f32[16,256,1,256]{3,2,0,1:T(1,128)} %broadcast_select_fusion.2, s32[]{:T(128)} %constant.196.clone.1, s32[]{:T(128)} %constant.196.clone.1, s32[]{:T(128)} %constant.196.clone.1, s32[]{:T(128)} %constant.196.clone.1) | dynamic-update-slice | bytes 8388612 | tf_op jit(solution)/shard_map/scatter | solution.py:97
  2358.0 22.9 copy.178
  (85 shorter events, 7.6 us)
Async XLA Ops:
  6.5 257.3 %copy-start = (s32[8]{0:T(128)S(1)}, s32[8]{0:T(128)}, u32[]{:S(2)}) copy-start(s32[8]{0:T(128)} %param.11) | copy-start | bytes 100
  38.4 190.7 %all-to-all-start = ((f32[2,4,4,256,512]{4,3,2,0,1:T(8,128)}), f32[2,4,4,256,512]{4,3,2,0,1:T(8,128)}, u32[]{:S(2)}, u32[]{:S(2)}) async-start(f32[2,4,4,256,512]{4,3,2,0,1:T(8,128)} %copy.152), calls=%async_computation | async-start | bytes 33554432 | tf_op jit(solution)/shard_map/all_to_all | solution.py:40
  255.6 6.8 copy-start.2
  255.6 369.6 %all-to-all-start.1 = ((f32[8,1,4,256,512]{4,3,2,1,0:T(8,128)}), f32[8,1,4,256,512]{4,3,2,1,0:T(8,128)}, u32[]{:S(2)}, u32[]{:S(2)}) async-start(f32[8,1,4,256,512]{4,3,2,1,0:T(8,128)} %fusion.2), calls=%async_computation.1 | async-start | bytes 33554432 | tf_op jit(solution)/shard_map/all_to_all | solution.py:48
  261.5 843.1 %all-gather.15.cloned.1.call-start = ((), (), s32[]{:S(2)}) async-start(), calls=%async_computation.4 | async-start | bytes 37748736 | tf_op jit(solution)/shard_map/all_gather | solution.py:11
  817.9 360.4 %all-gather.11.cloned.1.call-start = ((), (), s32[]{:S(2)}) async-start(), calls=%async_computation.2 | async-start | bytes 1310720 | tf_op jit(solution)/shard_map/all_gather | solution.py:11
  1129.8 15.2 copy-start.10
  1150.4 2.0 copy-start.6
  1153.4 325.4 %all-gather.17.cloned.1.call-start = ((), (), s32[]{:S(2)}) async-start(), calls=%async_computation.5 | async-start | bytes 37748736 | tf_op jit(solution)/shard_map/all_gather | solution.py:11
  1190.0 337.7 %all-gather.13.cloned.1.call-start = ((), (), s32[]{:S(2)}) async-start(), calls=%async_computation.3 | async-start | bytes 1310720 | tf_op jit(solution)/shard_map/all_gather | solution.py:11
  1499.6 2.1 copy-start.3
  1502.7 324.0 %all-gather.19.cloned.1.call-start = ((), (), s32[]{:S(2)}) async-start(), calls=%async_computation.6 | async-start | bytes 37748736 | tf_op jit(solution)/shard_map/all_gather | solution.py:11
  1537.9 567.7 %all-gather.21.cloned.1.call-start = ((), (), s32[]{:S(2)}) async-start(), calls=%async_computation.7 | async-start | bytes 31457280 | tf_op jit(solution)/shard_map/all_gather | solution.py:11
  1842.0 7.5 copy-start.4
  1842.0 7.5 copy-start.7
  1847.6 1.9 copy-start.9
  1879.5 0.8 copy-start.11
  2105.6 20.7 copy-start.5
  2105.6 20.7 copy-start.8
  2358.0 22.9 copy-start.1
Sparse Core Ops, SparseCore 0:
  818.1 286.5 all-gather.14
  1153.5 24.8 all-gather.10
  1190.1 288.6 all-gather.16
  1502.8 24.8 all-gather.12
  1538.0 288.6 all-gather.18
  1879.7 225.8 all-gather.20
